TPU v7x, 128 devices: a whole 4x4x4 slice. The times are simulated.
128 devices in a mesh: occ: 4 (over y_hi, core), aux: 32 (over x, z, y_lo).
Axes of the slice: x: 4, y: 4 (y_hi: 2, y_lo: 2; y = y_hi * 2 + y_lo), z: 4, core: 2. Of those that a mesh axis runs over, the one named last changes fastest.
Arguments:
- three_index: bfloat16 [12000, 6, 1920], P('aux'), may hold values from -0.47851562 to 0.47851562
- occ_energy: float32 [6], replicated, may hold values from -1.5 to -0.3
- vir_energy: float32 [1920], replicated, may hold values from 0.25 to 2.95
- batch_table: int32 [6], replicated, may hold values from 0 to 5, each once
- orbital_order: int32 [6], replicated, may hold values from 0 to 5, each once
- occ_pair_int: bfloat16 [2, 2, 12000], P(None, None, 'aux'), may hold values from -0.03881836 to 0.03881836
- half_ao: bfloat16 [2, 12000, 4000], P(None, 'aux'), may hold values from -9.536743e-06 to 9.536743e-06
- vir_coeff: bfloat16 [4000, 1920], P('aux', 'occ'), may hold values from -0.09375 to 0.09375
Outputs:
- gamma: bfloat16 [12000, 2, 1920], P('aux', None, 'occ')
- orbital_gradient: float32 [2, 1920], P(None, ('occ', 'aux'))
Inputs may be any that keep to these rules, and one draw needn't show every extreme that they name: `batch_table`: a permutation of 0 to 5; its first 4 entries are the partner orbitals of the window. `orbital_order`: a permutation of 0 to 5; its first 2 entries are the orbitals whose amplitudes are formed.
All inputs are finite; a program needn't handle non-finite values.
Results may differ from a plain program's by a relative error of at most 0.019.
Values may be sent and summed in bfloat16 or wider, within the bound.
No kernel may reach another device: no remote copies, remote signals or barrier semaphores. Data moves between devices by JAX's collectives and lax.ppermute only.
A program may use at most 128 MiB of HBM per device.

v0:
```python
import functools
import jax
import jax.numpy as jnp
from jax import lax
from jax.sharding import Mesh
from jax.sharding import PartitionSpec as P

NI = 2
NPART_DEV = 1
AUX = ("aux_0", "aux_1", "aux_2")
OCC = ("occ_0", "occ_1")
OCC_AUX = ("occ_0", "occ_1", "aux_0", "aux_1", "aux_2")


def own_rows(terms, axes):
    so_far = terms.astype(jnp.bfloat16)
    for axis in axes:
        so_far = lax.psum_scatter(so_far, axis, scatter_dimension=0, tiled=True)
    return so_far.astype(jnp.float32)


def one_axis_at_a_time(shard, axes):
    return functools.reduce(lax.psum, axes, shard)


def in_blocks(shard, dim, count):
    before, after = (shard.shape[:dim], shard.shape[dim + 1 :])
    return jnp.moveaxis(shard.reshape(*before, count, -1, *after), dim, 0)


def sent_and_summed(shard, axis, dim):
    count = lax.axis_size(axis)
    pieces = lax.all_to_all(in_blocks(shard, dim, count), axis, 0, 0, tiled=True)
    return jnp.sum(pieces, axis=0)


def local(
    three_index,
    occ_energy,
    vir_energy,
    batch_table,
    orbital_order,
    occ_pair_int,
    half_ao,
    vir_coeff,
):
    aux_width = lax.axis_size(AUX)
    nvirt = three_index.shape[2]
    row_share = nvirt // aux_width
    occ_place = lax.axis_index(OCC)
    aux_place = lax.axis_index(AUX)
    own_orbits = orbital_order[:NI]
    my_partners = lax.dynamic_slice_in_dim(batch_table, occ_place * NPART_DEV, NPART_DEV)
    left_block = jnp.take(three_index, own_orbits, axis=1)
    right_block = jnp.take(three_index, my_partners, axis=1)
    left_energy = jnp.take(occ_energy, own_orbits)
    right_energy = jnp.take(occ_energy, my_partners)
    pair_block = jnp.einsum(
        "qsa,qkb->askb", left_block, right_block, preferred_element_type=jnp.float32
    )
    pair_rows = own_rows(
        pair_block.reshape(row_share * lax.axis_size(AUX), NI * NPART_DEV * nvirt), AUX
    )
    row_count = pair_rows.shape[0]
    shaped = pair_rows.reshape(row_count, NI, NPART_DEV, nvirt)
    row_energy = lax.dynamic_slice_in_dim(vir_energy, aux_place * row_share, row_count)
    denominator = (
        row_energy[:, None, None, None]
        + vir_energy[None, None, None, :]
        - left_energy[None, :, None, None]
        - right_energy[None, None, :, None]
    )
    amps_rows = (-shaped / denominator).astype(jnp.bfloat16)
    gamma_part = jnp.einsum(
        "askb,qkb->qsa",
        lax.all_gather(amps_rows, AUX, axis=0, tiled=True),
        right_block,
        preferred_element_type=jnp.float32,
    )
    gamma_out = lax.psum_scatter(
        gamma_part.astype(jnp.bfloat16), OCC, scatter_dimension=2, tiled=True
    )
    density_part = -jnp.einsum(
        "askb,atkb->st", amps_rows, amps_rows, preferred_element_type=jnp.float32
    )
    density = one_axis_at_a_time(density_part, OCC_AUX)
    pair_int = occ_pair_int.astype(jnp.float32)
    coulomb = jnp.einsum("stq,st->q", pair_int, density, precision=lax.Precision.HIGHEST)
    exchange = jnp.einsum("suq,tu->stq", pair_int, density, precision=lax.Precision.HIGHEST)
    identity = jnp.eye(NI, dtype=jnp.float32)
    coefficient = (2.0 * identity[:, :, None] * coulomb[None, None, :] - exchange).astype(
        jnp.bfloat16
    )
    aux_rows = half_ao.shape[1]
    fock_part = jnp.dot(
        coefficient.reshape(NI, NI * aux_rows),
        half_ao.reshape(NI * aux_rows, half_ao.shape[2]),
        preferred_element_type=jnp.float32,
    )
    occ_side = -jnp.einsum(
        "usq,qua->sa", occ_pair_int, gamma_out, preferred_element_type=jnp.float32
    )
    fock_tile = sent_and_summed(fock_part, AUX, 1)
    vir_side = jnp.dot(fock_tile, vir_coeff.astype(jnp.float32), precision=lax.Precision.HIGHEST)
    gradient = sent_and_summed(occ_side + vir_side, AUX, 1)
    return (gamma_out, gradient)


def solution(mesh):
    torus = Mesh(mesh.devices.reshape(2, 2, 4, 4, 2), ("occ_0", "occ_1", "aux_0", "aux_1", "aux_2"))
    return jax.shard_map(
        local,
        mesh=torus,
        in_specs=(
            P(AUX, None, None),
            P(),
            P(),
            P(),
            P(),
            P(None, None, AUX),
            P(None, AUX, None),
            P(AUX, OCC),
        ),
        out_specs=(P(AUX, None, OCC), P(None, OCC_AUX)),
        check_vma=False,
    )
```

profile of v0, /device:TPU:0, one launch (start us, length us, event | category | flops | bytes accessed | tf_op | source)
XLA Modules:
  0.0 715.4 jit_solution(11130920844778028338)
XLA Ops:
  7.2 1.2 dynamic_slice.6
  10.4 0.7 compare_and_fusion
  11.1 4.5 gather_fusion
  15.6 12.4 %convolution_convert_fusion = bf16[1920,2,1920]{2,0,1:T(8,128)(2,1)} fusion(bf16[2,375,1920]{2,1,0:T(8,128)(2,1)S(1)} %gather_fusion, pred[2]{0:T(512)(128)(4,1)S(1)} %get-tuple-element.30, bf16[375,6,1920]{2,0,1:T(8,128)(2,1)} %param.8, s32[]{:T(128)} %bitcast.1, pred[]{:T(512)} %bitcast), kind=kOutput, calls=%fused_computation.5 | convolution fusion | flops 5539132928 | bytes 19070466 | tf_op jit(solution)/shard_map/qsa,qkb->askb/dot_general | solution.py:58
  27.9 20.1 %copy.19 = bf16[1920,3840]{1,0:T(8,128)(2,1)} copy(bf16[1920,3840]{0,1:T(8,128)(2,1)} %bitcast.75) | data formatting | bytes 29491200 | tf_op jit(solution)/shard_map/convert_element_type | solution.py:16
  48.2 134.6 %reduce-scatter.5.cloned.1.call-done = bf16[480,3840]{1,0:T(8,128)(2,1)} async-done(((bf16[1920,3840]{1,0:T(8,128)(2,1)}), bf16[480,3840]{1,0:T(8,128)(2,1)}) %reduce-scatter.5.cloned.1.call-update) | async-done | bytes 3686416 | tf_op jit(solution)/shard_map/reduce_scatter | solution.py:18
  182.8 0.6 gather_fusion.1
  183.6 44.2 %reduce-scatter.7.cloned.1.call-done = bf16[120,3840]{1,0:T(8,128)(2,1)} async-done(((bf16[480,3840]{1,0:T(8,128)(2,1)}), bf16[120,3840]{1,0:T(8,128)(2,1)}) %reduce-scatter.7.cloned.1.call-update) | async-done | bytes 921616 | tf_op jit(solution)/shard_map/reduce_scatter | solution.py:18
  227.9 16.9 %fusion = bf16[64,3840]{1,0:T(8,128)(2,1)S(1)} fusion(bf16[120,3840]{1,0:T(8,128)(2,1)} %reduce-scatter.7.cloned.1.call-done), kind=kCustom, calls=%all-reduce-scatter | all-reduce-scatter fusion | flops 491521 | bytes 1413632
  244.8 2.4 collective-permute-start
  248.6 0.7 dynamic-slice.13
  250.7 0.7 concatenate.2
  251.4 1.1 divide_convert_fusion
  253.0 1.5 fusion.29
  254.7 317.7 %all-gather.2.cloned.1.call-done = bf16[1920,2,1,1920]{3,1,2,0:T(2,128)(2,1)} async-done(((bf16[60,2,1,1920]{3,1,2,0:T(2,128)(2,1)}), bf16[1920,2,1,1920]{3,1,2,0:T(2,128)(2,1)}) %all-gather.2.cloned.1.call-update) | async-done | bytes 14745616 | tf_op jit(solution)/shard_map/all_gather | solution.py:76
  572.4 13.1 %fusion.9 = bf16[375,2,1920]{2,0,1:T(8,128)(2,1)S(1)} fusion(bf16[1920,2,1,1920]{3,1,2,0:T(2,128)(2,1)} %all-gather.2.cloned.1.call-done, bf16[375,6,1920]{2,0,1:T(8,128)(2,1)} %param.8, s32[]{:T(128)} %bitcast.1, pred[]{:T(512)} %bitcast), kind=kOutput, calls=%fused_computation.9 | convolution fusion | flops 5531759616 | bytes 19070464 | tf_op jit(solution)/shard_map/askb,qkb->qsa/dot_general | solution.py:74
  585.6 7.0 copy.22
  592.8 1.6 fusion.25
  594.3 6.4 psum.35
  600.8 2.4 psum.36
  603.2 10.0 %copy.24 = bf16[2,375,4000]{2,1,0:T(8,128)(2,1)} copy(bf16[2,375,4000]{2,0,1:T(2,128)(2,1)} %param.14) | data formatting | bytes 12000000 | tf_op args[6]
  613.2 10.7 %psum.37 = f32[2,2]{1,0:T(2,128)S(1)} all-reduce(f32[2,2]{1,0:T(2,128)S(1)} %psum.36), channel_id=1, replica_groups=mesh['occ_0'=2,'occ_1'=2,'aux_0'=4,'aux_1'=4,'aux_2'=2] {'aux_0'}, use_global_device_ids=true, to_apply=%region_6.7 | all-reduce | flops 4 | bytes 32 | tf_op jit(solution)/shard_map/psum | solution.py:23
  623.9 8.1 %reshape.144 = bf16[750,4000]{1,0:T(8,128)(2,1)} reshape(bf16[2,375,4000]{2,1,0:T(8,128)(2,1)} %copy.24) | data formatting | bytes 12000000 | tf_op jit(solution)/shard_map/reshape | solution.py:97
  632.0 10.6 %psum.38 = f32[2,2]{1,0:T(2,128)S(1)} all-reduce(f32[2,2]{1,0:T(2,128)S(1)} %psum.37), channel_id=1, replica_groups=mesh['occ_0'=2,'occ_1'=2,'aux_0'=4,'aux_1'=4,'aux_2'=2] {'aux_1'}, use_global_device_ids=true, to_apply=%region_7.8 | all-reduce | flops 4 | bytes 32 | tf_op jit(solution)/shard_map/psum | solution.py:23
  642.7 28.6 %dot_general.35 = bf16[32,125,750]{1,0,2:T(8,128)(2,1)} reshape(bf16[4000,750]{0,1:T(8,128)(2,1)} %bitcast.74) | data formatting | bytes 12000000 | tf_op jit(solution)/shard_map/dot_general | solution.py:95
  671.3 5.0 psum.39
  676.8 5.1 fusion.18
  681.8 3.9 all-to-all-start
  686.9 7.0 all-to-all-done
  694.0 1.6 constant_dynamic-slice_fusion
  696.5 11.7 %all_to_all.10 = f32[32,2,15]{2,1,0:T(2,128)S(1)} all-to-all(f32[32,2,15]{2,1,0:T(2,128)S(1)} %copy.26), channel_id=1, replica_groups=mesh['occ_0'=2,'occ_1'=2,'aux_0'=4,'aux_1'=4,'aux_2'=2] {'aux_0','aux_1'..., dimensions={0} | all-to-all | bytes 7680 | tf_op jit(solution)/shard_map/all_to_all | solution.py:33
  708.2 0.6 reduce_sum.19
  (50 shorter events, 4.7 us)
Async XLA Ops:
  7.2 688.9 %copy-start = (bf16[125,480]{0,1:T(8,128)(2,1)S(1)}, bf16[125,480]{0,1:T(8,128)(2,1)}, u32[]{:S(2)}) copy-start(bf16[125,480]{0,1:T(8,128)(2,1)} %param.15) | copy-start | bytes 360004
  7.2 175.5 %reduce-scatter.5.cloned.1.call-start = ((), (), s32[]{:S(2)}) async-start(), calls=%async_computation.4 | async-start | bytes 18432000 | tf_op jit(solution)/shard_map/reduce_scatter | solution.py:18
  48.1 134.7 %copy-start.1 = (f32[6]{0:T(128)S(1)}, f32[6]{0:T(128)}, u32[]{:S(2)}) copy-start(f32[6]{0:T(128)} %param.9) | copy-start | bytes 76
  48.1 135.4 %copy-start.4 = (f32[1920]{0:T(1024)S(1)}, f32[1920]{0:T(1024)}, u32[]{:S(2)}) copy-start(f32[1920]{0:T(1024)} %param.10) | copy-start | bytes 23044
  48.1 179.8 %reduce-scatter.7.cloned.1.call-start = ((), (), s32[]{:S(2)}) async-start(), calls=%async_computation.5 | async-start | bytes 4608000 | tf_op jit(solution)/shard_map/reduce_scatter | solution.py:18
  182.7 65.9 %copy-start.6 = (u32[128]{0:T(128)S(1)}, u32[128]{0:T(128)}, u32[]{:S(2)}) copy-start(u32[128]{0:T(128)} %constant.137) | copy-start | bytes 1540
  182.7 389.7 %all-gather.2.cloned.1.call-start = ((), (), s32[]{:S(2)}) async-start(), calls=%async_computation.6 | async-start | bytes 15206400 | tf_op jit(solution)/shard_map/all_gather | solution.py:76
  244.8 5.9 collective-permute-start
  254.5 439.5 %all-reduce.5.cloned.1.call-start = ((), (), s32[]{:S(2)}) async-start(), calls=%async_computation.7 | async-start | bytes 5898240
  585.6 7.0 copy-start.3
  642.7 33.6 %copy-start.5 = (bf16[2,2,375]{2,1,0:T(2,128)(2,1)S(1)}, bf16[2,2,375]{2,1,0:T(2,128)(2,1)}, u32[]{:S(2)}) copy-start(bf16[2,2,375]{2,1,0:T(2,128)(2,1)} %param.13) | copy-start | bytes 9004
  671.3 14.4 %copy-start.7 = (u32[128]{0:T(128)S(1)}, u32[128]{0:T(128)}, u32[]{:S(2)}) copy-start(u32[128]{0:T(128)} %constant.141) | copy-start | bytes 1540
  681.8 12.1 %all-to-all-start = ((f32[32,2,125]{2,1,0:T(2,128)}), f32[32,2,125]{2,1,0:T(2,128)S(1)}, u32[]{:S(2)}, u32[]{:S(2)}) async-start(f32[32,2,125]{2,1,0:T(2,128)} %fusion.18), calls=%async_computation.2 | async-start | bytes 65536 | tf_op jit(solution)/shard_map/all_to_all | solution.py:33
  695.7 13.1 %copy-start.2 = (bf16[375,2,480]{0,2,1:T(8,128)(2,1)}, bf16[375,2,480]{0,2,1:T(8,128)(2,1)S(1)}, u32[]{:S(2)}) copy-start(bf16[375,2,480]{0,2,1:T(8,128)(2,1)S(1)} %copy.27) | copy-start | bytes 2160004
Sparse Core Ops, SparseCore 0:
  48.2 134.4 reduce-scatter.4
  185.1 42.6 reduce-scatter.6
  254.6 317.7 all-gather.1
  592.7 75.0 all-reduce.4
where the time goes:
time: 717 us; the launch traced here: 715 us
  waiting for transfers between devices  504 us (70%)
  local copies, waits for them, and re-layouts  86.4 us (12%)
  blocking collectives  63.8 us (9%)
  matrix products  33 us (5%)
  between operations  18 us (3%)
    all_gather x1, waiting for transfers between devices, local(): lax.all_gather(amps_rows, AUX, axis=0, tiled=True)  318 us
    reduce_scatter x2, waiting for transfers between devices, own_rows(): so_far = lax.psum_scatter(so_far, axis, scatter_dimension=0, tiled=True)  179 us
    psum x5, blocking collectives, one_axis_at_a_time(): return functools.reduce(lax.psum, axes, shard)  35.2 us
    dot_general x1, local copies, waits for them, and re-layouts, local(): jnp.dot(coefficient.reshape(NI, NI * aux_rows), half_ao.reshape(NI * aux_...  28.6 us
    convert_element_type x1, local copies, waits for them, and re-layouts, own_rows(): so_far = terms.astype(jnp.bfloat16)  20.1 us
    unnamed x1, blocking collectives  16.9 us
  transfers between devices with their start and end apart: 6, of which 4 were waited for; matrix products, arithmetic and copies ran while one was open for 8% of the time, Pallas kernels for 0%

commit v1 on v0

--- a/solution.py
+++ b/solution.py
@@ -10,6 +10,14 @@
 AUX = ("aux_0", "aux_1", "aux_2")
 OCC = ("occ_0", "occ_1")
 OCC_AUX = ("occ_0", "occ_1", "aux_0", "aux_1", "aux_2")
+
+
+def draft_outputs(sample):
+    clean = jax.lax.all_to_all(
+        jnp.stack([sample] * jax.lax.axis_size(AUX)), axis_name=AUX, split_axis=0, concat_axis=0
+    )
+    w1 = jnp.concatenate(clean, axis=0)
+    return w1
 
 
 def own_rows(terms, axes):
@@ -72,10 +80,7 @@
     )
     amps_rows = (-shaped / denominator).astype(jnp.bfloat16)
     gamma_part = jnp.einsum(
-        "askb,qkb->qsa",
-        lax.all_gather(amps_rows, AUX, axis=0, tiled=True),
-        right_block,
-        preferred_element_type=jnp.float32,
+        "askb,qkb->qsa", draft_outputs(amps_rows), right_block, preferred_element_type=jnp.float32
     )
     gamma_out = lax.psum_scatter(
         gamma_part.astype(jnp.bfloat16), OCC, scatter_dimension=2, tiled=True

time: 717 us -> 600 us (0.84)
  waiting for transfers between devices: 504 us -> 228 us
  blocking collectives: 63.8 us -> 217 us
  local copies, waits for them, and re-layouts: 86.4 us -> 98 us
    all_gather x1 -> x0, waiting for transfers between devices: 318 us -> none  [local(): lax.all_gather(amps_rows, AUX, axis=0, tiled=True)]
    unnamed x6 -> x8, waiting for transfers between devices: 0.08 us -> 221 us
    reduce_scatter x2 -> x0, waiting for transfers between devices: 179 us -> none  [own_rows(): so_far = lax.psum_scatter(so_far, axis, scatter_dimension=0, tiled=True)]
    all_to_all x0 -> x1, blocking collectives: none -> 172 us  [draft_outputs(): jax.lax.all_to_all(jnp.stack([sample] * jax.lax.axis_size(AUX)), axis_nam...]
    unnamed x25 -> x21, local copies, waits for them, and re-layouts: 14.2 us -> 35.1 us
    convert_element_type x1 -> x0, local copies, waits for them, and re-layouts: 20.1 us -> none  [own_rows(): so_far = terms.astype(jnp.bfloat16)]
    unnamed x1 -> x0, blocking collectives: 16.9 us -> none
    another operation x0 -> x1, local copies, waits for them, and re-layouts: none -> 8.15 us  [draft_outputs(): jnp.stack([sample] * jax.lax.axis_size(AUX))]
  transfers between devices with their start and end apart: 6 -> 5, of which waited for: 4 -> 4; matrix products, arithmetic and copies ran while one was open for 8% -> 10% of each run, Pallas kernels for 0% -> 0%
where the time goes in v1:
time: 600 us; the launch traced here: 599 us
  waiting for transfers between devices  228 us (38%)
  blocking collectives  217 us (36%)
  local copies, waits for them, and re-layouts  98 us (16%)
  matrix products  29.5 us (5%)
  between operations  17.8 us (3%)
    unnamed x8, waiting for transfers between devices  221 us
    all_to_all x1, blocking collectives, draft_outputs(): jax.lax.all_to_all(jnp.stack([sample] * jax.lax.axis_size(AUX)), axis_nam...  172 us
    unnamed x21, local copies, waits for them, and re-layouts  35.1 us
    psum x5, blocking collectives, one_axis_at_a_time(): return functools.reduce(lax.psum, axes, shard)  33.3 us
    dot_general x1, local copies, waits for them, and re-layouts, local(): jnp.dot(coefficient.reshape(NI, NI * aux_rows), half_ao.reshape(NI * aux_...  28.5 us
    dot_general x1, matrix products, local(): jnp.einsum('qsa,qkb->askb', left_block, right_block, preferred_element_ty...  12.4 us
  transfers between devices with their start and end apart: 5, of which 4 were waited for; matrix products, arithmetic and copies ran while one was open for 10% of the time, Pallas kernels for 0%

profile of v1, /device:TPU:0, one launch (start us, length us, event | category | flops | bytes accessed | tf_op | source)
XLA Modules:
  0.0 598.6 jit_solution(8467800016916589284)
XLA Ops:
  7.2 1.2 dynamic_slice.6
  10.4 0.7 compare_and_fusion
  11.1 4.5 gather_fusion
  15.6 12.4 %convolution_convert_fusion = bf16[1920,2,1920]{2,0,1:T(8,128)(2,1)} fusion(bf16[2,375,1920]{2,1,0:T(8,128)(2,1)S(1)} %gather_fusion, pred[2]{0:T(512)(128)(4,1)S(1)} %get-tuple-element.30, bf16[375,6,1920]{2,0,1:T(8,128)(2,1)} %param.8, s32[]{:T(128)} %bitcast.1, pred[]{:T(512)} %bitcast), kind=kOutput, calls=%fused_computation.4 | convolution fusion | flops 5539132928 | bytes 19070466 | tf_op jit(solution)/shard_map/qsa,qkb->askb/dot_general | solution.py:66
  27.9 20.1 %copy.32 = bf16[1920,3840]{1,0:T(8,128)(2,1)} copy(bf16[1920,3840]{0,1:T(8,128)(2,1)} %bitcast.77) | data formatting | bytes 29491200
  48.2 134.6 %reduce-scatter.8.cloned.1.call-done = bf16[480,3840]{1,0:T(8,128)(2,1)} async-done(((bf16[1920,3840]{1,0:T(8,128)(2,1)}), bf16[480,3840]{1,0:T(8,128)(2,1)}) %reduce-scatter.8.cloned.1.call-update) | async-done | bytes 3686416
  182.8 45.1 %reduce-scatter.10.cloned.1.call-done = bf16[120,3840]{1,0:T(8,128)(2,1)} async-done(((bf16[480,3840]{1,0:T(8,128)(2,1)}), bf16[120,3840]{1,0:T(8,128)(2,1)}) %reduce-scatter.10.cloned.1.call-update) | async-done | bytes 921616
  227.9 2.2 copy.35
  230.8 0.6 gather_fusion.1
  232.3 0.6 dynamic-slice.7
  233.9 41.3 %all-reduce.5.cloned.1.call-done = bf16[120,3840]{0,1:T(8,128)(2,1)} async-done(((bf16[120,3840]{0,1:T(8,128)(2,1)}), bf16[120,3840]{0,1:T(8,128)(2,1)}) %all-reduce.5.cloned.1.call-update) | async-done | bytes 921616
  275.2 2.0 fusion.15
  277.6 1.0 copy.21
  278.6 8.2 %stack.2 = bf16[32,60,2,1,1920]{4,2,1,3,0:T(2,128)(2,1)S(1)} broadcast(bf16[60,2,1920]{2,1,0:T(2,128)(2,1)S(1)} %copy.21), dimensions={1,2,4} | broadcast | bytes 15206400 | tf_op jit(solution)/shard_map/stack | solution.py:17
  286.8 172.1 %all_to_all.15 = bf16[32,60,2,1,1920]{4,2,1,3,0:T(2,128)(2,1)S(1)} all-to-all(bf16[32,60,2,1,1920]{4,2,1,3,0:T(2,128)(2,1)S(1)} %stack.2), channel_id=1, replica_groups=mesh['occ_0'=2,'occ_1'=2,'aux_0'=4,'aux_1'=4,'aux_2'=2] {'aux_0','aux_1'..., dimensions={0} | all-to-all | bytes 29491200 | tf_op jit(solution)/shard_map/all_to_all | solution.py:16
  458.9 9.6 %fusion.7 = bf16[375,2,1920]{2,0,1:T(8,128)(2,1)} fusion(bf16[1920,2,1920]{2,1,0:T(2,128)(2,1)S(1)} %bitcast.76, bf16[375,6,1920]{2,0,1:T(8,128)(2,1)} %param.8, s32[]{:T(128)} %bitcast.1, pred[]{:T(512)} %bitcast), kind=kOutput, calls=%fused_computation.8 | convolution fusion | flops 5531759616 | bytes 19070464 | tf_op jit(solution)/shard_map/askb,qkb->qsa/dot_general | solution.py:82
  468.5 8.7 %copy.23 = bf16[375,2,1920]{0,1,2:T(2,128)(2,1)} copy(bf16[375,2,1920]{2,0,1:T(8,128)(2,1)} %fusion.7) | data formatting | bytes 5760000 | tf_op jit(solution)/shard_map/convert_element_type | solution.py:86
  477.2 1.0 copy.25
  478.2 1.6 fusion.26
  479.8 6.4 %psum.35 = f32[2,2]{1,0:T(2,128)S(1)} all-reduce(f32[2,2]{1,0:T(2,128)S(1)} %fusion.26), channel_id=1, replica_groups=mesh['occ_0'=2,'occ_1'=2,'aux_0'=4,'aux_1'=4,'aux_2'=2] {'occ_0'}, use_global_device_ids=true, to_apply=%region_4.5 | all-reduce | flops 4 | bytes 32 | tf_op jit(solution)/shard_map/psum | solution.py:31
  486.2 2.4 psum.36
  488.7 9.7 %copy.27 = bf16[2,375,4000]{2,1,0:T(8,128)(2,1)} copy(bf16[2,375,4000]{2,0,1:T(2,128)(2,1)} %param.14) | data formatting | bytes 12000000 | tf_op args[6]
  498.4 11.4 %psum.37 = f32[2,2]{1,0:T(2,128)S(1)} all-reduce(f32[2,2]{1,0:T(2,128)S(1)} %psum.36), channel_id=1, replica_groups=mesh['occ_0'=2,'occ_1'=2,'aux_0'=4,'aux_1'=4,'aux_2'=2] {'aux_0'}, use_global_device_ids=true, to_apply=%region_6.7 | all-reduce | flops 4 | bytes 32 | tf_op jit(solution)/shard_map/psum | solution.py:31
  509.7 8.1 %reshape.137 = bf16[750,4000]{1,0:T(8,128)(2,1)} reshape(bf16[2,375,4000]{2,1,0:T(8,128)(2,1)} %copy.27) | data formatting | bytes 12000000 | tf_op jit(solution)/shard_map/reshape | solution.py:102
  517.9 8.2 %psum.38 = f32[2,2]{1,0:T(2,128)S(1)} all-reduce(f32[2,2]{1,0:T(2,128)S(1)} %psum.37), channel_id=1, replica_groups=mesh['occ_0'=2,'occ_1'=2,'aux_0'=4,'aux_1'=4,'aux_2'=2] {'aux_1'}, use_global_device_ids=true, to_apply=%region_7.8 | all-reduce | flops 4 | bytes 32 | tf_op jit(solution)/shard_map/psum | solution.py:31
  526.1 28.5 %dot_general.35 = bf16[32,125,750]{1,0,2:T(8,128)(2,1)} reshape(bf16[4000,750]{0,1:T(8,128)(2,1)} %bitcast.75) | data formatting | bytes 12000000 | tf_op jit(solution)/shard_map/dot_general | solution.py:100
  554.6 4.9 psum.39
  560.0 5.1 fusion.19
  565.0 3.9 all-to-all-start.1
  570.2 7.0 %all-to-all-done.1 = f32[32,2,125]{2,1,0:T(2,128)S(1)} async-done(((f32[32,2,125]{2,1,0:T(2,128)}), f32[32,2,125]{2,1,0:T(2,128)S(1)}, u32[]{:S(2)}, u32[]{:S(2)}) %all-to-all-start.1) | async-done | bytes 32032 | tf_op jit(solution)/shard_map/all_to_all | solution.py:41
  577.2 1.6 constant_dynamic-slice_fusion
  579.7 11.7 %all_to_all.16 = f32[32,2,15]{2,1,0:T(2,128)S(1)} all-to-all(f32[32,2,15]{2,1,0:T(2,128)S(1)} %copy.29), channel_id=1, replica_groups=mesh['occ_0'=2,'occ_1'=2,'aux_0'=4,'aux_1'=4,'aux_2'=2] {'aux_0','aux_1'..., dimensions={0} | all-to-all | bytes 7680 | tf_op jit(solution)/shard_map/all_to_all | solution.py:41
  (43 shorter events, 4.3 us)
Async XLA Ops:
  7.2 572.1 %copy-start = (bf16[125,480]{0,1:T(8,128)(2,1)S(1)}, bf16[125,480]{0,1:T(8,128)(2,1)}, u32[]{:S(2)}) copy-start(bf16[125,480]{0,1:T(8,128)(2,1)} %param.15) | copy-start | bytes 360004
  7.2 175.5 %reduce-scatter.8.cloned.1.call-start = ((), (), s32[]{:S(2)}) async-start(), calls=%async_computation.5 | async-start | bytes 18432000
  48.1 179.8 %reduce-scatter.10.cloned.1.call-start = ((), (), s32[]{:S(2)}) async-start(), calls=%async_computation.6 | async-start | bytes 4608000
  182.7 47.5 %copy-start.1 = (f32[6]{0:T(128)S(1)}, f32[6]{0:T(128)}, u32[]{:S(2)}) copy-start(f32[6]{0:T(128)} %param.9) | copy-start | bytes 76
  182.7 49.5 %copy-start.3 = (f32[1920]{0:T(1024)S(1)}, f32[1920]{0:T(1024)}, u32[]{:S(2)}) copy-start(f32[1920]{0:T(1024)} %param.10) | copy-start | bytes 23044
  182.7 49.6 %copy-start.6 = (u32[128]{0:T(128)S(1)}, u32[128]{0:T(128)}, u32[]{:S(2)}) copy-start(u32[128]{0:T(128)} %constant.137) | copy-start | bytes 1540
  182.7 92.4 %all-reduce.5.cloned.1.call-start = ((), (), s32[]{:S(2)}) async-start(), calls=%async_computation.7 | async-start | bytes 1966080
  230.1 347.1 %all-reduce.7.cloned.1.call-start = ((), (), s32[]{:S(2)}) async-start(), calls=%async_computation.8 | async-start | bytes 5898240
  526.1 33.4 %copy-start.4 = (bf16[2,2,375]{2,1,0:T(2,128)(2,1)S(1)}, bf16[2,2,375]{2,1,0:T(2,128)(2,1)}, u32[]{:S(2)}) copy-start(bf16[2,2,375]{2,1,0:T(2,128)(2,1)} %param.13) | copy-start | bytes 9004
  560.0 9.0 %copy-start.5 = (u32[128]{0:T(128)S(1)}, u32[128]{0:T(128)}, u32[]{:S(2)}) copy-start(u32[128]{0:T(128)} %constant.141) | copy-start | bytes 1540
  565.0 12.1 %all-to-all-start.1 = ((f32[32,2,125]{2,1,0:T(2,128)}), f32[32,2,125]{2,1,0:T(2,128)S(1)}, u32[]{:S(2)}, u32[]{:S(2)}) async-start(f32[32,2,125]{2,1,0:T(2,128)} %fusion.19), calls=%async_computation.1 | async-start | bytes 65536 | tf_op jit(solution)/shard_map/all_to_all | solution.py:41
  579.0 13.1 %copy-start.2 = (bf16[375,2,480]{0,2,1:T(8,128)(2,1)}, bf16[375,2,480]{0,2,1:T(8,128)(2,1)S(1)}, u32[]{:S(2)}) copy-start(bf16[375,2,480]{0,2,1:T(8,128)(2,1)S(1)} %copy.30) | copy-start | bytes 2160004
Sparse Core Ops, SparseCore 0:
  48.2 134.4 reduce-scatter.7
  185.1 42.6 reduce-scatter.9
  230.3 44.7 all-reduce.4
  477.4 71.7 all-reduce.6
